TPU v7x, 128 devices: a whole 4x4x4 slice. The times are simulated.
128 devices in a mesh: tower: 2 (over z_hi), grp: 2 (over core), seq: 32 (over y, x, z_lo).
Axes of the slice: x: 4, y: 4, z: 4 (z_hi: 2, z_lo: 2; z = z_hi * 2 + z_lo), core: 2. Of those that a mesh axis runs over, the one named last changes fastest.
Arguments:
- queries: bfloat16 [2, 8192, 3072], P('tower', 'seq', 'grp'), may hold values from -15 to 15, as said below
- keys: bfloat16 [2, 8192, 3072], P('tower', 'seq', 'grp'), may hold values from -6 to 6, as said below
- values: bfloat16 [2, 8192, 3072], P('tower', 'seq', 'grp'), may hold values from -6 to 6
- stamps: int32 [2, 8192], P('tower', 'seq'), may hold values from 0 to 8191, as said below
- partner: int32 [32], replicated, may hold values from 0 to 31, as said below
- w_out: bfloat16 [2, 3072, 3072], P('tower', 'grp'), may hold values from -0.109375 to 0.109375
Outputs:
- mixed_out: bfloat16 [2, 8192, 3072], P('tower', 'seq', 'grp')
Inputs may be any that keep to these rules, and one draw needn't show every extreme that they name: queries are bounded as stated. keys are bounded as stated. Video frames are runs of 1560 consecutive video rows starting at multiples of 1560; every video token's stamp is the first row index of its frame, so a frame may span several shards. The audio tokens at shard position partner[s] carry the distinct stamps s * 256 to (s + 1) * 256 - 1. partner is a permutation of the 32 shard positions.
All inputs are finite; a program needn't handle non-finite values.
Results may differ from a plain program's by a relative error of at most 0.015.
Values may be sent and summed in bfloat16 or wider, within the bound.
A program may use at most 256 MiB of HBM per device.

v0:
```python
import math

import jax
import jax.numpy as jnp
from jax import lax
from jax.sharding import PartitionSpec as P

HEAD = 128


def from_partner(block, axis, apart):
    count = lax.axis_size(axis)
    route = []
    for low in range(count):
        high = low | 1 << apart
        if high != low and high < count:
            route += [(low, high), (high, low)]
    return lax.ppermute(block, axis, route)


def rotate(inputs, times):
    row_count = inputs.shape[0]
    half_size = HEAD // 2
    frequency = jnp.exp(-math.log(10000.0) * jnp.arange(half_size, dtype=jnp.float32) / half_size)
    angles = times.astype(jnp.float32)[:, None] * frequency[None, :]
    cosine = jnp.cos(angles)[:, None, :]
    sine_part = jnp.sin(angles)[:, None, :]
    halves = inputs.astype(jnp.float32).reshape(row_count, -1, 2, half_size)
    first_half = halves[:, :, 0]
    second_half = halves[:, :, 1]
    turned = jnp.stack(
        [
            first_half * cosine - second_half * sine_part,
            first_half * sine_part + second_half * cosine,
        ],
        axis=2,
    )
    return turned.reshape(row_count, -1).astype(jnp.bfloat16)


def opened(fragment):
    return (fragment[0], fragment[1])


def absorb(softmax_state, query_heads, key_block, value_block):
    old_max, denominator, numerator = softmax_state
    head_count = query_heads.shape[1]
    key_heads = key_block.reshape(key_block.shape[0], head_count, HEAD)
    value_heads = value_block.reshape(value_block.shape[0], head_count, HEAD)
    scores = jnp.einsum(
        "qhd,khd->hqk", query_heads, key_heads, preferred_element_type=jnp.float32
    ) * (1.0 / math.sqrt(HEAD))
    new_max = jnp.maximum(old_max, jnp.max(scores, axis=-1))
    exponent = jnp.exp(scores - new_max[:, :, None])
    rescale = jnp.exp(old_max - new_max)
    denominator = denominator * rescale + jnp.sum(exponent, axis=-1)
    weights = exponent.astype(jnp.bfloat16)
    numerator = numerator * rescale[:, :, None] + jnp.einsum(
        "hqk,khd->hqd", weights, value_heads, preferred_element_type=jnp.float32
    )
    return (new_max, denominator, numerator)


def finish(softmax_state):
    old_max, denominator, numerator = softmax_state
    result = numerator / denominator[:, :, None]
    return jnp.transpose(result, (1, 0, 2)).reshape(result.shape[1], -1)


def body(queries, keys, values, stamps, partner, w_out):
    tok_rows = queries.shape[1]
    columns = queries.shape[2]
    head_count = columns // HEAD
    own_queries = rotate(queries[0], stamps[0]).reshape(tok_rows, head_count, HEAD)
    tower_index = lax.axis_index("tower")
    seq_place = lax.axis_index("seq")
    seq_count = lax.axis_size("seq")
    shards = jnp.arange(seq_count, dtype=jnp.int32)
    inverse_here = jnp.sum(jnp.where(partner == seq_place, shards, 0))
    chosen = jnp.where(tower_index == 1, partner[seq_place], inverse_here)
    payload = (rotate(keys[0], stamps[0]), values[0])
    start_state = (
        jnp.full((head_count, tok_rows), -1e30, jnp.float32),
        jnp.zeros((head_count, tok_rows), jnp.float32),
        jnp.zeros((head_count, tok_rows, HEAD), jnp.float32),
    )
    gathered = (
        lax.all_gather(payload[0], "seq", axis=0, tiled=True),
        lax.all_gather(payload[1], "seq", axis=0, tiled=True),
    )
    all_keys, all_values = opened(gathered)
    rounds = seq_count // 8
    block_rows = 8 * tok_rows

    def absorb_block(softmax_state, block_pair):
        return (absorb(softmax_state, own_queries, block_pair[0], block_pair[1]), None)

    softmax_state, unused = lax.scan(
        absorb_block,
        start_state,
        (
            all_keys.reshape(rounds, block_rows, columns),
            all_values.reshape(rounds, block_rows, columns),
        ),
    )
    pair_keys = lax.dynamic_slice_in_dim(all_keys, chosen * tok_rows, tok_rows, 0)
    pair_values = lax.dynamic_slice_in_dim(all_values, chosen * tok_rows, tok_rows, 0)
    self_out = finish(softmax_state)
    cross_keys, cross_values = from_partner((pair_keys, pair_values), "tower", 0)
    cross_out = finish(absorb(start_state, own_queries, cross_keys, cross_values))
    combined = (self_out + cross_out).astype(jnp.bfloat16)
    partial_value = jnp.dot(combined, w_out[0], preferred_element_type=jnp.float32)
    mixed_out = lax.psum_scatter(
        partial_value.astype(jnp.bfloat16), "grp", scatter_dimension=1, tiled=True
    )
    return mixed_out[None]


def solution(mesh):
    return jax.shard_map(
        body,
        mesh=mesh,
        in_specs=(
            P("tower", "seq", "grp"),
            P("tower", "seq", "grp"),
            P("tower", "seq", "grp"),
            P("tower", "seq"),
            P(),
            P("tower", "grp", None),
        ),
        out_specs=P("tower", "seq", "grp"),
        check_vma=False,
    )
```

profile of v0, /device:TPU:1, one launch (start us, length us, event | category | flops | bytes accessed | tf_op | source)
XLA Modules:
  0.0 1453.9 jit_solution(11782532578303659679)
XLA Ops:
  15.2 559.0 %all-gather.4.cloned.1.call-done = bf16[8192,1536]{0,1:T(8,128)(2,1)} async-done(((bf16[256,1536]{0,1:T(8,128)(2,1)}), bf16[8192,1536]{0,1:T(8,128)(2,1)}) %all-gather.4.cloned.1.call-update) | async-done | bytes 25165840 | tf_op jit(solution)/shard_map/all_gather | solution.py:88
  576.3 14.9 %collective-permute-start = (bf16[256,1536]{0,1:T(8,128)(2,1)}, bf16[256,1536]{0,1:T(8,128)(2,1)}, u32[]{:S(2)}, u32[]{:S(2)}) collective-permute-start(bf16[256,1536]{0,1:T(8,128)(2,1)} %constant_dynamic-slice_fusion.2), channel_id=1, source_target_pairs={{0,64},{64,0},{1,65},{65,1},{2,66},{66,2},{3,67},{67,3},{4,68},{68... | collective-permute-start | bytes 2359304 | tf_op jit(solution)/shard_map/ppermute | solution.py:18
  591.2 560.4 %all-gather.6.cloned.1.call-done = bf16[1,8192,1536]{2,1,0:T(8,128)(2,1)} async-done(((bf16[1,256,1536]{2,1,0:T(8,128)(2,1)}), bf16[1,8192,1536]{2,1,0:T(8,128)(2,1)}) %all-gather.6.cloned.1.call-update) | async-done | bytes 25165840 | tf_op jit(solution)/shard_map/all_gather | solution.py:89
  1156.2 20.9 %copy.36 = bf16[192,4,8,2048]{3,2,0,1:T(8,128)(2,1)} copy(bf16[192,4,8,2048]{3,2,1,0:T(8,128)(2,1)} %bitcast.81) | data formatting | bytes 50331648 | tf_op jit(solution)/shard_map/reshape | solution.py:102
  1177.2 235.8 %while.15 = (s32[]{:T(128)}, f32[12,256]{1,0:T(8,128)S(1)}, f32[12,256]{1,0:T(8,128)S(1)}, f32[12,256,128]{2,1,0:T(8,128)S(1)}, bf16[4,2048,1536]{1,2,0:T(8,128)...) while((s32[]{:T(128)}, f32[12,256]{1,0:T(8,128)S(1)}, ...), condition=%wide.region_3.4_spmd.clone, body=%wide.region_0.3_spmd.clone.sunk | while | flops 3272752128 | bytes 129958000 | solution.py:98
  1182.9 8.6 copy.38
  1191.5 6.5 constant_dynamic-slice_fusion.5
  1198.1 14.6 %bitcast_reduce_fusion.2 = (f32[12,256]{1,0:T(8,128)S(1)}, f32[12,2048,256]{2,1,0:T(8,128)}) fusion(bf16[2048,12,128]{0,2,1:T(8,128)(2,1)} %bitcast.77, bf16[256,12,128]{2,0,1:T(8,128)(2,1)S(1)} %get-tuple-element.180), kind=kOutput, calls=%fused_computation.1.clone.1 | convolution fusion | flops 1623192576 | bytes 32256000 | tf_op jit(solution)/shard_map/while/body/eval_jaxpr/qhd,khd->hqk/dot_general | solution.py:50
  1212.7 10.5 fusion.48
  1223.1 12.9 fusion.50
  1241.9 8.6 copy.38
  1257.0 14.6 %bitcast_reduce_fusion.2 = (f32[12,256]{1,0:T(8,128)S(1)}, f32[12,2048,256]{2,1,0:T(8,128)}) fusion(bf16[2048,12,128]{0,2,1:T(8,128)(2,1)} %bitcast.77, bf16[256,12,128]{2,0,1:T(8,128)(2,1)S(1)} %get-tuple-element.180), kind=kOutput, calls=%fused_computation.1.clone.1 | convolution fusion | flops 1623192576 | bytes 32256000 | tf_op jit(solution)/shard_map/while/body/eval_jaxpr/qhd,khd->hqk/dot_general | solution.py:50
  1271.6 10.5 fusion.48
  1282.1 12.9 fusion.50
  1300.9 8.6 copy.38
  1316.0 14.6 %bitcast_reduce_fusion.2 = (f32[12,256]{1,0:T(8,128)S(1)}, f32[12,2048,256]{2,1,0:T(8,128)}) fusion(bf16[2048,12,128]{0,2,1:T(8,128)(2,1)} %bitcast.77, bf16[256,12,128]{2,0,1:T(8,128)(2,1)S(1)} %get-tuple-element.180), kind=kOutput, calls=%fused_computation.1.clone.1 | convolution fusion | flops 1623192576 | bytes 32256000 | tf_op jit(solution)/shard_map/while/body/eval_jaxpr/qhd,khd->hqk/dot_general | solution.py:50
  1330.6 10.5 fusion.48
  1341.1 12.9 fusion.50
  1359.8 8.6 copy.38
  1375.0 14.6 %bitcast_reduce_fusion.2 = (f32[12,256]{1,0:T(8,128)S(1)}, f32[12,2048,256]{2,1,0:T(8,128)}) fusion(bf16[2048,12,128]{0,2,1:T(8,128)(2,1)} %bitcast.77, bf16[256,12,128]{2,0,1:T(8,128)(2,1)S(1)} %get-tuple-element.180), kind=kOutput, calls=%fused_computation.1.clone.1 | convolution fusion | flops 1623192576 | bytes 32256000 | tf_op jit(solution)/shard_map/while/body/eval_jaxpr/qhd,khd->hqk/dot_general | solution.py:50
  1389.5 10.5 fusion.48
  1400.0 12.9 fusion.50
  1422.0 7.5 fusion.14
  1429.5 17.8 %reduce-scatter.2.cloned.1.call-done = bf16[256,1536]{1,0:T(8,128)(2,1)} async-done(((bf16[256,3072]{1,0:T(8,128)(2,1)}), bf16[256,1536]{1,0:T(8,128)(2,1)}) %reduce-scatter.2.cloned.1.call-update) | async-done | bytes 786448 | tf_op jit(solution)/shard_map/reduce_scatter | solution.py:113
  (59 shorter events, 65.6 us)
Async XLA Ops:
  6.5 2.4 copy-start.1
  6.5 567.7 %all-gather.4.cloned.1.call-start = ((), (), s32[]{:S(2)}) async-start(), calls=%async_computation.1 | async-start | bytes 25952256 | tf_op jit(solution)/shard_map/all_gather | solution.py:88
  9.7 2.3 copy-start.2
  11.2 1140.5 %all-gather.6.cloned.1.call-start = ((), (), s32[]{:S(2)}) async-start(), calls=%async_computation.3 | async-start | bytes 25952256 | tf_op jit(solution)/shard_map/all_gather | solution.py:89
  11.9 1435.4 %reduce-scatter.2.cloned.1.call-start = ((), (), s32[]{:S(2)}) async-start(), calls=%async_computation.2 | async-start | bytes 2359296 | tf_op jit(solution)/shard_map/reduce_scatter | solution.py:113
  14.8 1162.4 %copy-start = (bf16[256,12,2,64]{0,3,2,1:T(8,128)(2,1)}, bf16[256,12,2,64]{0,3,2,1:T(8,128)(2,1)S(1)}, u32[]{:S(2)}) copy-start(bf16[256,12,2,64]{0,3,2,1:T(8,128)(2,1)S(1)} %pad_maximum_fusion.1) | copy-start | bytes 2359300
  576.3 838.3 %collective-permute-start = (bf16[256,1536]{0,1:T(8,128)(2,1)}, bf16[256,1536]{0,1:T(8,128)(2,1)}, u32[]{:S(2)}, u32[]{:S(2)}) collective-permute-start(bf16[256,1536]{0,1:T(8,128)(2,1)} %constant_dynamic-slice_fusion.2), channel_id=1, source_target_pairs={{0,64},{64,0},{1,65},{65,1},{2,66},{66,2},{3,67},{67,3},{4,68},{68... | collective-permute-start | bytes 2359304 | tf_op jit(solution)/shard_map/ppermute | solution.py:18
  1153.7 263.5 %collective-permute-start.1 = (bf16[256,1536]{1,0:T(8,128)(2,1)}, bf16[256,1536]{1,0:T(8,128)(2,1)}, u32[]{:S(2)}, u32[]{:S(2)}) collective-permute-start(bf16[256,1536]{1,0:T(8,128)(2,1)} %dynamic-slice_bitcast_fusion), channel_id=1, source_target_pairs={{0,64},{64,0},{1,65},{65,1},{2,66},{66,2},{3,67},{67,3},{4,68},{68... | collective-permute-start | bytes 2359304 | tf_op jit(solution)/shard_map/ppermute | solution.py:18
Sparse Core Ops, SparseCore 0:
  11.3 562.8 all-gather.3
  575.9 575.7 all-gather.5
  1429.6 17.6 reduce-scatter.1
where the time goes:
time: 1460 us; the launch traced here: 1450 us
  waiting for transfers between devices  1140 us (78%)
  matrix products  122 us (8%)
  local copies, waits for them, and re-layouts  115 us (8%)
  other arithmetic  46.1 us (3%)
  starting transfers between devices  17.5 us (1%)
  between operations  14.6 us (1%)
    all_gather x1, waiting for transfers between devices, body(): lax.all_gather(payload[1], 'seq', axis=0, tiled=True)  560 us
    all_gather x1, waiting for transfers between devices, body(): lax.all_gather(payload[0], 'seq', axis=0, tiled=True)  559 us
    dynamic_slice x12, local copies, waits for them, and re-layouts, body(): lax.scan(absorb_block, start_state, (all_keys.reshape(rounds, block_rows,...  83.7 us
    dot_general x5, matrix products, absorb(): jnp.einsum('qhd,khd->hqk', query_heads, key_heads, preferred_element_type...  60.3 us
    dot_general x5, matrix products, absorb(): jnp.einsum('hqk,khd->hqd', weights, value_heads, preferred_element_type=j...  54.2 us
    reduce_sum x5, other arithmetic, absorb(): denominator = denominator * rescale + jnp.sum(exponent, axis=-1)  42.4 us
  transfers between devices with their start and end apart: 5, of which 3 were waited for; matrix products, arithmetic and copies ran while one was open for 18% of the time, Pallas kernels for 0%

commit v1 on v0

v1 whole, which is shorter than its diff:
```python
import functools
import math

import jax
import jax.numpy as jnp
from jax import lax
from jax.experimental import pallas as pl
from jax.experimental.pallas import tpu as pltpu
from jax.sharding import PartitionSpec as P

HEAD = 128
TOK = 256
PHASES = 3
BLOCKS = 32
ROWS = 4 * TOK
MODEL = 3072
HALF = MODEL // 2
TILE = 512
SCALE = 1.0 / (math.sqrt(HEAD) * math.log(2.0))
F32 = jnp.float32
BF16 = jnp.bfloat16
MESH = pl.DeviceIdType.MESH

ALONG_X = (False, True, False)

ORDER = (
    (0, 0), (1, 0), (0, 1), (2, 0), (0, 2), (0, 3),
    (1, 1), (1, 2), (1, 3), (2, 1), (2, 2), (2, 3),
)
AHEAD = {
    ("below", 1): 8, ("above", 1): 8,
    ("below", 2): 16, ("above", 2): 16,
    ("cross", 0): 11, ("finish", 0): 15, ("project", 0): 18,
    ("cross", 1): 17, ("finish", 1): 21, ("project", 1): 22,
}
NEEDS = {
    (0, 0): ("own",), (0, 1): ("sib0",),
    (1, 0): ("below",), (1, 1): ("above",),
    (2, 0): ("sib1",), (2, 1): ("sib2",),
    (3, 0): ("opposite",), (3, 1): ("sib3",),
}


def plan():
    steps = [(phase, part, half) for phase, part in ORDER for half in range(2)]
    at = {}
    for place, (phase, part, half) in enumerate(steps):
        for event in NEEDS[(part, half)]:
            at[(event, phase)] = max(place - 1, -1)
            if event == "own":
                at[("ask", phase)] = max(place - 1, -1)
    at[("cross", 2)] = at[("sib3", 2)]
    for key, place in AHEAD.items():
        at[key] = place if key not in at else min(place, at[key])
    rank = ["ask", "own", "below", "above", "opposite", "sib0", "sib1", "sib2", "sib3",
            "cross", "finish", "project"]
    slots = {}
    for (event, phase), place in sorted(at.items(), key=lambda e: (e[1], rank.index(e[0][0]), e[0][1])):
        slots.setdefault(place, []).append((event, phase))
    return slots


def pick(index, values):
    chosen = jnp.int32(values[0])
    for place in range(1, len(values)):
        chosen = jnp.where(index == place, jnp.int32(values[place]), chosen)
    return chosen


def kernel(
    q_hbm, k_hbm, v_hbm, cos_ref, sin_ref, chosen_ref, w_hbm, out_ref,
    q_raw, k_raw, v_raw, w_ref, q_stage, kv_stage, kv, q_here, q_far, cross_mine, cross_far,
    picked, joined, home, total, part_out, part_in,
    acc, top, block_top, scores, weights,
    load_sem, kv_s, kv_r, q_s, q_r, line_s, line_r, opp_s, opp_r, sib_s, sib_r,
    far_s, far_r, cross_s, cross_r, home_s, home_r, part_s, part_r,
):
    t = lax.axis_index("tower")
    c = lax.axis_index("grp")
    s = lax.axis_index("seq")
    y, x, zl = s // 8, (s // 2) % 4, s % 2
    p = zl + t - 2 * zl * t

    def place(along_x, u, w, z):
        return w * 8 + u * 2 + z if along_x else u * 8 + w * 2 + z

    class Line:
        def __init__(self, along_x):
            self.along_x = along_x
            self.u, self.w = (x, y) if along_x else (y, x)
            self.a, self.wl = self.w // 2, self.w % 2
            self.r = self.wl * 2 + zl
            self.gl = self.wl * 2 + p
            self.i = 2 * self.w + zl
            self.mine = c == self.a

        def peer(self, r):
            return (t, self.a, place(self.along_x, self.u, 2 * c + r // 2, r % 2))

        def next(self, step):
            return (t, c, place(self.along_x, (self.u + step) % 4, self.w, zl))

        def chunk(self, step, core):
            return ((self.u + step) % 4) * 8 + 4 * core

    lines = {False: Line(False), True: Line(True)}
    sibling = (t, 1 - c, s)
    far = (1 - t, c, s + 1 - 2 * zl)

    def remote(src, dst, send, recv, device):
        return pltpu.make_async_remote_copy(
            src_ref=src, dst_ref=dst, send_sem=send, recv_sem=recv,
            device_id=device, device_id_type=MESH,
        )

    loads = [
        pltpu.make_async_copy(k_hbm.at[0], k_raw, load_sem.at[0]),
        pltpu.make_async_copy(v_hbm.at[0], v_raw, load_sem.at[1]),
        pltpu.make_async_copy(q_hbm.at[0], q_raw, load_sem.at[2]),
        pltpu.make_async_copy(w_hbm.at[0], w_ref, load_sem.at[3]),
    ]
    for load in loads:
        load.start()

    barrier = pltpu.get_barrier_semaphore()

    def greet(device):
        pl.semaphore_signal(barrier, inc=1, device_id=device, device_id_type=MESH)

    count = jnp.int32(6)
    for line in lines.values():
        for r in range(4):
            @pl.when(jnp.logical_not(jnp.logical_and(line.mine, line.r == r)))
            def _():
                greet(line.peer(r))
        greet(line.next(1))
        greet(line.next(3))
        count = count + 4 - jnp.where(line.mine, 1, 0)
    greet(sibling)
    greet(far)

    def turned(raw, head):
        entries = raw[:, pl.ds(pl.multiple_of(head * HEAD, HEAD), HEAD)].astype(F32)
        swapped = pltpu.roll(entries, HEAD // 2, 1)
        return (entries * cos_ref[...] + swapped * sin_ref[...]).astype(BF16)

    def deliver(phase, gl, src, dst, send, recv):
        line = lines[ALONG_X[phase]]
        r = (gl // 2) * 2 + (gl % 2 + t - 2 * (gl % 2) * t)
        here = jnp.logical_and(line.mine, line.r == r)

        @pl.when(here)
        def _():
            pltpu.make_async_copy(src, dst, recv).start()

        @pl.when(jnp.logical_not(here))
        def _():
            remote(src, dst, send, recv, line.peer(r)).start()

    def prepare_kv(phase):
        line = lines[ALONG_X[phase]]

        def one(gl, _):
            head = gl * PHASES + phase
            kv_stage[phase * 4 + gl, 0] = turned(k_raw, head)
            kv_stage[phase * 4 + gl, 1] = v_raw[:, pl.ds(pl.multiple_of(head * HEAD, HEAD), HEAD)]
            return 0

        lax.fori_loop(0, 4, one, 0)

    def send_kv(phase):
        line = lines[ALONG_X[phase]]
        for gl in range(4):
            deliver(phase, gl, kv_stage.at[phase * 4 + gl],
                    kv.at[phase * BLOCKS + line.u * 8 + line.i],
                    kv_s.at[phase * 4 + gl], kv_r.at[phase * 4 + line.r])

    def send_q(phase):
        line = lines[ALONG_X[phase]]

        def one(gl, _):
            q_stage[phase * 4 + gl] = turned(q_raw, gl * PHASES + phase)
            return 0

        lax.fori_loop(0, 4, one, 0)
        for gl in range(4):
            deliver(phase, gl, q_stage.at[phase * 4 + gl], q_here.at[phase * 4 + line.r],
                    q_s.at[phase * 4 + gl], q_r.at[phase * 4 + line.r])

    loads[0].wait()
    loads[1].wait()
    prepare_kv(0)
    pl.semaphore_wait(barrier, count)
    send_kv(0)
    loads[2].wait()
    send_q(0)
    prepare_kv(1)
    send_kv(1)
    send_q(1)
    prepare_kv(2)
    send_kv(2)
    send_q(2)

    acc[...] = jnp.zeros(acc.shape, F32)
    top[...] = jnp.full(top.shape, -1e30, F32)

    def blocks(phase, first, size):
        return kv.at[pl.ds(phase * BLOCKS + first, size)]

    def landed(dst, recv):
        remote(dst, dst, recv, recv, sibling).wait_recv()

    def to_sibling(phase, number, part):
        remote(part, part, sib_s.at[phase * 4 + number], sib_r.at[phase * 4 + number], sibling).start()

    def event(name, phase):
        line = lines[ALONG_X[phase]]
        if name == "ask":
            for r in range(4):
                landed(q_here.at[phase * 4 + r], q_r.at[phase * 4 + r])
            remote(q_here.at[pl.ds(phase * 4, 4)], q_far.at[pl.ds(phase * 4, 4)],
                   far_s.at[phase], far_r.at[phase], far).start()
        elif name == "own":
            first = line.chunk(0, c)
            for r in range(4):
                landed(kv.at[phase * BLOCKS + first + r], kv_r.at[phase * 4 + r])
            part = blocks(phase, first, 4)
            remote(part, part, line_s.at[phase * 2], line_r.at[phase * 2], line.next(1)).start()
            remote(part, part, line_s.at[phase * 2 + 1], line_r.at[phase * 2 + 1], line.next(3)).start()
            to_sibling(phase, 0, part)
        elif name == "below":
            first = line.chunk(3, c)
            part = blocks(phase, first, 4)
            landed(part, line_r.at[phase * 2])
            passed = blocks(phase, first, 2)
            remote(passed, passed, opp_s.at[phase * 2], opp_r.at[phase * 2], line.next(1)).start()
            to_sibling(phase, 1, part)
        elif name == "above":
            first = line.chunk(1, c)
            part = blocks(phase, first, 4)
            landed(part, line_r.at[phase * 2 + 1])
            passed = blocks(phase, first + 2, 2)
            remote(passed, passed, opp_s.at[phase * 2 + 1], opp_r.at[phase * 2 + 1], line.next(3)).start()
            to_sibling(phase, 2, part)
        elif name == "opposite":
            first = line.chunk(2, c)
            landed(blocks(phase, first, 2), opp_r.at[phase * 2])
            landed(blocks(phase, first + 2, 2), opp_r.at[phase * 2 + 1])
            to_sibling(phase, 3, blocks(phase, first, 4))
        elif name[:3] == "sib":
            number = int(name[3])
            step = (0, 3, 1, 2)[number]
            landed(blocks(phase, line.chunk(step, 1 - c), 4), sib_r.at[phase * 4 + number])
        elif name == "cross":
            cross(phase)
        elif name == "finish":
            finish(phase)
        else:
            project(phase)

    def cross(phase):
        kind = 4 if ALONG_X[phase] else 0
        want = [chosen_ref[kind + r] for r in range(4)]

        def select(step, _):
            rows = pl.ds(pl.multiple_of((step % 8) * 32, 32), 32)
            which = step // 8
            found = [jnp.zeros((32, HEAD), BF16) for r in range(4)]
            for block in range(BLOCKS):
                entries = kv[phase * BLOCKS + block, which, rows, :]
                for r in range(4):
                    found[r] = jnp.where(want[r] == block, entries, found[r])
            for r in range(4):
                picked[r, which, rows, :] = found[r]
            return 0

        lax.fori_loop(0, 16, select, 0)
        landed(q_far.at[pl.ds(phase * 4, 4)], far_r.at[phase])

        def one(r, _):
            found = lax.dot_general(
                q_far[phase * 4 + r], picked[r, 0], (((1,), (1,)), ((), ())),
                preferred_element_type=F32,
            ) * SCALE
            exponent = jnp.exp2(found - jnp.max(found, axis=1, keepdims=True))
            denominator = jnp.sum(exponent, axis=1, keepdims=True)
            numerator = jnp.dot(exponent.astype(BF16), picked[r, 1], preferred_element_type=F32)
            cross_mine[phase * 4 + r] = (numerator / denominator).astype(BF16)
            return 0

        lax.fori_loop(0, 4, one, 0)
        remote(cross_mine.at[pl.ds(phase * 4, 4)], cross_far.at[pl.ds(phase * 4, 4)],
               cross_s.at[phase], cross_r.at[phase], far).start()

    def finish(phase):
        line = lines[ALONG_X[phase]]
        landed(cross_far.at[pl.ds(phase * 4, 4)], cross_r.at[phase])
        for r in range(4):
            rows = pl.ds(phase * ROWS + r * TOK, TOK)
            own = acc[rows, 0:HEAD] / acc[rows, HEAD:]
            joined[phase * 4 + r] = (own + cross_far[phase * 4 + r].astype(F32)).astype(BF16)
            here = jnp.logical_and(line.mine, line.r == r)
            src, dst = joined.at[phase * 4 + r], home.at[phase * 4 + line.gl]
            recv = home_r.at[phase * 4 + line.gl]

            @pl.when(here)
            def _():
                pltpu.make_async_copy(src, dst, recv).start()

            @pl.when(jnp.logical_not(here))
            def _():
                remote(src, dst, home_s.at[phase * 4 + r], recv, line.peer(r)).start()

    def product(phase, columns):
        left = jnp.concatenate([home[phase * 4 + gl] for gl in range(4)], axis=1)
        right = jnp.concatenate(
            [w_ref[(gl * PHASES + phase) * HEAD:(gl * PHASES + phase + 1) * HEAD, columns]
             for gl in range(4)], axis=0)
        return jnp.dot(left, right, preferred_element_type=F32)

    def home_landed(phase):
        for gl in range(4):
            landed(home.at[phase * 4 + gl], home_r.at[phase * 4 + gl])

    def project(phase):
        home_landed(phase)
        if phase == 0:
            loads[3].wait()

        def one(n, _):
            columns = pl.ds(pl.multiple_of(n * TILE, TILE), TILE)
            value = product(phase, columns)
            total[:, columns] = value if phase == 0 else total[:, columns] + value
            return 0

        lax.fori_loop(0, MODEL // TILE, one, 0)

    def qk(phase, first, slot):
        rows = pl.ds(pl.multiple_of(phase * 4, 4), 4)
        queries = q_here[rows].reshape(ROWS, HEAD)
        keys = kv[pl.ds(phase * BLOCKS + first, 4), 0].reshape(ROWS, HEAD)
        found = lax.dot_general(
            queries, keys, (((1,), (1,)), ((), ())), preferred_element_type=F32
        )
        scores[slot] = found
        most = found[:, 0:HEAD]
        for column in range(1, ROWS // HEAD):
            most = jnp.maximum(most, found[:, column * HEAD:(column + 1) * HEAD])
        block_top[slot] = jnp.broadcast_to(
            jnp.max(most, axis=1, keepdims=True) * SCALE, (ROWS, HEAD)
        )

    def absorb(phase, first, slot):
        rows = pl.ds(pl.multiple_of(phase * ROWS, ROWS), ROWS)
        old_top = top[rows, :]
        new_top = jnp.maximum(old_top, block_top[slot])
        top[rows, :] = new_top
        for column in range(ROWS // HEAD):
            columns = slice(column * HEAD, (column + 1) * HEAD)
            weights[slot, :, columns] = jnp.exp2(
                scores[slot, :, columns] * SCALE - new_top
            ).astype(BF16)
        values = kv[pl.ds(phase * BLOCKS + first, 4), 1].reshape(ROWS, HEAD)
        widened = jnp.concatenate([values, jnp.ones_like(values)], axis=1)
        added = jnp.dot(weights[slot], widened, preferred_element_type=F32)
        rescale = jnp.exp2(old_top - new_top)
        acc[rows, :] = acc[rows, :] * jnp.concatenate([rescale, rescale], axis=1) + added

    def where_is(phase, part, half):
        u = jnp.where(pick(phase, [int(f) for f in ALONG_X]) == 1, x, y)
        step = jnp.where(part == 0, 0, jnp.where(part == 3, 2, 1 if half else 3))
        other = 1 - c
        split = other if half else c
        core = jnp.where(part == 1, c, jnp.where(part == 2, other, split))
        return ((u + step) % 4) * 8 + 4 * core

    slots = plan()
    phases = [phase for phase, part in ORDER]
    parts = [part for phase, part in ORDER]

    def events_of(pair, half):
        for number in range(len(ORDER)):
            todo = slots.get(2 * number + half, [])
            if todo:
                @pl.when(pair == number)
                def _(todo=todo):
                    for name, phase in todo:
                        event(name, phase)

    for name, phase in slots.get(-1, []):
        event(name, phase)
    qk(phases[0], where_is(jnp.int32(phases[0]), jnp.int32(parts[0]), 0), 0)

    def pair_step(pair, _):
        following = jnp.minimum(pair + 1, len(ORDER) - 1)
        phase, part = pick(pair, phases), pick(pair, parts)
        later_phase, later_part = pick(following, phases), pick(following, parts)
        events_of(pair, 0)
        qk(phase, where_is(phase, part, 1), 1)
        absorb(phase, where_is(phase, part, 0), 0)
        events_of(pair, 1)
        qk(later_phase, where_is(later_phase, later_part, 0), 0)
        absorb(phase, where_is(phase, part, 1), 1)
        return 0

    lax.fori_loop(0, len(ORDER), pair_step, 0)

    finish(2)
    home_landed(2)
    theirs, ours = (1 - c) * HALF, c * HALF

    def for_sibling(n, _):
        columns = pl.ds(pl.multiple_of(theirs + n * TILE, TILE), TILE)
        here = pl.ds(pl.multiple_of(n * TILE, TILE), TILE)
        part_out[:, here] = (total[:, columns] + product(2, columns)).astype(BF16)
        return 0

    lax.fori_loop(0, HALF // TILE, for_sibling, 0)
    exchange = remote(part_out, part_in, part_s, part_r, sibling)
    exchange.start()

    def for_us(n, _):
        columns = pl.ds(pl.multiple_of(ours + n * TILE, TILE), TILE)
        total[:, columns] = total[:, columns] + product(2, columns)
        return 0

    lax.fori_loop(0, HALF // TILE, for_us, 0)
    exchange.wait()

    def emit(n, _):
        columns = pl.ds(pl.multiple_of(ours + n * TILE, TILE), TILE)
        here = pl.ds(pl.multiple_of(n * TILE, TILE), TILE)
        out_ref[0, :, here] = (total[:, columns] + part_in[:, here].astype(F32)).astype(BF16)
        return 0

    lax.fori_loop(0, HALF // TILE, emit, 0)

    def sent(src, send):
        remote(src, src, send, send, sibling).wait_send()

    for phase in range(PHASES):
        line = lines[ALONG_X[phase]]
        for number in range(4):
            r = (number // 2) * 2 + (number % 2 + t - 2 * (number % 2) * t)

            @pl.when(jnp.logical_not(jnp.logical_and(line.mine, line.r == r)))
            def _():
                sent(kv_stage.at[phase * 4 + number], kv_s.at[phase * 4 + number])
                sent(q_stage.at[phase * 4 + number], q_s.at[phase * 4 + number])

            @pl.when(jnp.logical_not(jnp.logical_and(line.mine, line.r == number)))
            def _():
                sent(joined.at[phase * 4 + number], home_s.at[phase * 4 + number])

            sent(blocks(phase, 0, 4), sib_s.at[phase * 4 + number])
        for number in range(2):
            sent(blocks(phase, 0, 4), line_s.at[phase * 2 + number])
            sent(blocks(phase, 0, 2), opp_s.at[phase * 2 + number])
        sent(q_here.at[pl.ds(phase * 4, 4)], far_s.at[phase])
        sent(cross_mine.at[pl.ds(phase * 4, 4)], cross_s.at[phase])


def attention(queries, keys, values, cosine, sine, chosen, w_out):
    dma = pltpu.SemaphoreType.DMA
    anywhere = pl.BlockSpec(memory_space=pl.ANY)
    vmem = pl.BlockSpec(memory_space=pltpu.VMEM)
    heads = 4 * PHASES
    per_head = pltpu.VMEM((heads, TOK, HEAD), BF16)
    return pl.pallas_call(
        kernel,
        out_shape=jax.ShapeDtypeStruct((1, TOK, HALF), BF16),
        in_specs=[anywhere, anywhere, anywhere, vmem, vmem,
                  pl.BlockSpec(memory_space=pltpu.SMEM), anywhere],
        out_specs=vmem,
        scratch_shapes=[
            pltpu.VMEM((TOK, HALF), BF16),
            pltpu.VMEM((TOK, HALF), BF16),
            pltpu.VMEM((TOK, HALF), BF16),
            pltpu.VMEM((HALF, MODEL), BF16),
            per_head,
            pltpu.VMEM((heads, 2, TOK, HEAD), BF16),
            pltpu.VMEM((PHASES * BLOCKS, 2, TOK, HEAD), BF16),
            per_head, per_head, per_head, per_head,
            pltpu.VMEM((4, 2, TOK, HEAD), BF16),
            per_head, per_head,
            pltpu.VMEM((TOK, MODEL), F32),
            pltpu.VMEM((TOK, HALF), BF16),
            pltpu.VMEM((TOK, HALF), BF16),
            pltpu.VMEM((PHASES * ROWS, 2 * HEAD), F32),
            pltpu.VMEM((PHASES * ROWS, HEAD), F32),
            pltpu.VMEM((2, ROWS, HEAD), F32),
            pltpu.VMEM((2, ROWS, ROWS), F32),
            pltpu.VMEM((2, ROWS, ROWS), BF16),
            dma((4,)),
            dma((heads,)), dma((heads,)), dma((heads,)), dma((heads,)),
            dma((6,)), dma((6,)), dma((6,)), dma((6,)),
            dma((heads,)), dma((heads,)),
            dma((3,)), dma((3,)), dma((3,)), dma((3,)),
            dma((heads,)), dma((heads,)),
            dma, dma,
        ],
        compiler_params=pltpu.CompilerParams(
            collective_id=0, has_side_effects=True, vmem_limit_bytes=63 * 2**20
        ),
    )(queries, keys, values, cosine, sine, chosen, w_out)


def body(queries, keys, values, stamps, partner, w_out):
    half_size = HEAD // 2
    frequency = jnp.exp(-math.log(10000.0) * jnp.arange(half_size, dtype=F32) / half_size)
    angles = stamps[0].astype(F32)[:, None] * frequency[None, :]
    cosine, sine = jnp.cos(angles), jnp.sin(angles)
    cosine = jnp.concatenate([cosine, cosine], axis=1)
    sine = jnp.concatenate([-sine, sine], axis=1)
    t, c, s = lax.axis_index("tower"), lax.axis_index("grp"), lax.axis_index("seq")
    y, x = s // 8, (s // 2) % 4
    r = jnp.arange(4, dtype=jnp.int32)
    w, z = 2 * c + r // 2, r % 2
    asked = jnp.concatenate([y * 8 + w * 2 + z, w * 8 + x * 2 + z])
    shards = jnp.arange(BLOCKS, dtype=jnp.int32)[None, :]
    given = partner[None, :]
    forward = jnp.sum(jnp.where(shards == asked[:, None], given, 0), axis=1)
    inverse = jnp.sum(jnp.where(given == asked[:, None], shards, 0), axis=1)
    chosen = jnp.where(t == 1, forward, inverse)
    swapped = ((chosen // 2) % 4) * 8 + (chosen // 8) * 2 + chosen % 2
    chosen = jnp.where(jnp.arange(8) < 4, chosen, swapped).astype(jnp.int32)
    return attention(queries, keys, values, cosine, sine, chosen, w_out)


def solution(mesh):
    return jax.shard_map(
        body,
        mesh=mesh,
        in_specs=(
            P("tower", "seq", "grp"),
            P("tower", "seq", "grp"),
            P("tower", "seq", "grp"),
            P("tower", "seq"),
            P(),
            P("tower", "grp", None),
        ),
        out_specs=P("tower", "seq", "grp"),
        check_vma=False,
    )
```

time: 1460 us -> 112 us (0.08)
  waiting for transfers between devices: 1140 us -> 0 us
  matrix products: 122 us -> 0 us
  local copies, waits for them, and re-layouts: 115 us -> 2.06 us
  Pallas kernels: 0 us -> 106 us
  other arithmetic: 46.1 us -> 3.58 us
  starting transfers between devices: 17.5 us -> 0 us
    all_gather x2 -> x0, waiting for transfers between devices: 1120 us -> none  [the longest x1 560 us: body(): lax.all_gather(payload[1], 'seq', axis=0, tiled=True)]
    dot_general x11 -> x0, matrix products: 122 us -> none  [the longest x5 60.3 us: absorb(): jnp.einsum('qhd,khd->hqk', query_heads, key_heads, preferred_element_type...]
    pallas_call x0 -> x1, Pallas kernels: none -> 106 us  [attention(): pl.pallas_call(kernel, out_shape=jax.ShapeDtypeStruct((1, TOK, HALF), BF1...]
    dynamic_slice x15 -> x0, local copies, waits for them, and re-layouts: 88.5 us -> none  [the longest x12 83.7 us: body(): lax.scan(absorb_block, start_state, (all_keys.reshape(rounds, block_rows,...]
    reduce_sum x6 -> x1, other arithmetic: 43.1 us -> 0.87 us  [body(): inverse = jnp.sum(jnp.where(given == asked[:, None], shards, 0), axis=1)]
    reshape x1 -> x0, local copies, waits for them, and re-layouts: 20.9 us -> none  [body(): all_keys.reshape(rounds, block_rows, columns)]
    reduce_scatter x1 -> x0, waiting for transfers between devices: 17.8 us -> none  [body(): lax.psum_scatter(partial_value.astype(jnp.bfloat16), 'grp', scatter_dimen...]
    ppermute x2 -> x0, starting transfers between devices: 17.4 us -> none  [from_partner(): return lax.ppermute(block, axis, route)]
  transfers between devices with their start and end apart: 5 -> 0, of which waited for: 3 -> 0; matrix products, arithmetic and copies ran while one was open for 18% -> 0% of each run, Pallas kernels for 0% -> 0%
where the time goes in v1:
time: 112 us; the launch traced here: 111 us
  Pallas kernels  106 us (95%)
  other arithmetic  3.58 us (3%)
  local copies, waits for them, and re-layouts  2.06 us (2%)
    pallas_call x1, Pallas kernels, attention(): pl.pallas_call(kernel, out_shape=jax.ShapeDtypeStruct((1, TOK, HALF), BF1...  106 us

profile of v1, /device:TPU:1, one launch (start us, length us, event | category | flops | bytes accessed | tf_op | source)
XLA Modules:
  0.0 111.5 jit_solution(5986230287316451735)
XLA Ops:
  0.0 0.1 pad_add_fusion
  0.1 0.9 select_reduce_fusion
  1.0 0.6 compare_select_fusion.2.chosen_ref
  1.5 0.7 convert_element_type.10
  2.2 0.5 fusion
  2.8 0.8 pad_maximum_fusion
  3.6 105.8 %shard_map.64 = bf16[1,256,1536]{2,1,0:T(8,128)(2,1)} custom-call(bf16[1,256,1536]{2,1,0:T(8,128)(2,1)} %q_hbm.1, bf16[1,256,1536]{2,1,0:T(8,128)(2,1)} %k_hbm.1, bf16[1,256,1536]{2,1,0:T(8,128)(2,1)} %v_hbm.1, f32[256,128]{1,0:T(8,128)} %get-tuple-element.10.cos_ref, f32[256,128]{1,0:T(8,128)} %get-tuple-element.11.sin_ref, ...), custom_call_target="tpu_custom_call" | custom-call | tf_op jit(solution)/shard_map/pallas_call | solution.py:469
  109.4 2.1 %copy.8 = bf16[1,256,1536]{2,1,0:T(8,128)(2,1)} copy(bf16[1,256,1536]{2,1,0:T(8,128)(2,1)} %shard_map.64) | data formatting | bytes 1572864
  (2 shorter events, 0.0 us)

commit v2 on v1

--- a/solution.py
+++ b/solution.py
@@ -3,6 +3,7 @@
 
 import jax
 import jax.numpy as jnp
+import numpy as np
 from jax import lax
 from jax.experimental import pallas as pl
 from jax.experimental.pallas import tpu as pltpu
@@ -31,7 +32,7 @@
     ("below", 1): 8, ("above", 1): 8,
     ("below", 2): 16, ("above", 2): 16,
     ("cross", 0): 11, ("finish", 0): 15, ("project", 0): 18,
-    ("cross", 1): 17, ("finish", 1): 21, ("project", 1): 22,
+    ("cross", 1): 18, ("finish", 1): 21, ("project", 1): 22,
 }
 NEEDS = {
     (0, 0): ("own",), (0, 1): ("sib0",),
@@ -50,10 +51,13 @@
             if event == "own":
                 at[("ask", phase)] = max(place - 1, -1)
     at[("cross", 2)] = at[("sib3", 2)]
+    for phase in range(PHASES):
+        at[("near", phase)] = at[("sib2", phase)]
+        at[("rest", phase)] = at[("sib3", phase)]
     for key, place in AHEAD.items():
         at[key] = place if key not in at else min(place, at[key])
     rank = ["ask", "own", "below", "above", "opposite", "sib0", "sib1", "sib2", "sib3",
-            "cross", "finish", "project"]
+            "near", "rest", "cross", "finish", "project"]
     slots = {}
     for (event, phase), place in sorted(at.items(), key=lambda e: (e[1], rank.index(e[0][0]), e[0][1])):
         slots.setdefault(place, []).append((event, phase))
@@ -68,12 +72,13 @@
 
 
 def kernel(
-    q_hbm, k_hbm, v_hbm, cos_ref, sin_ref, chosen_ref, w_hbm, out_ref,
+    q_hbm, k_hbm, v_hbm, stamps_ref, frequency_ref, partner_ref, w_hbm, out_ref,
+    cos_ref, sin_ref,
     q_raw, k_raw, v_raw, w_ref, q_stage, kv_stage, kv, q_here, q_far, cross_mine, cross_far,
-    picked, joined, home, total, part_out, part_in,
+    held, joined, home, total, part_out, part_in,
     acc, top, block_top, scores, weights,
     load_sem, kv_s, kv_r, q_s, q_r, line_s, line_r, opp_s, opp_r, sib_s, sib_r,
-    far_s, far_r, cross_s, cross_r, home_s, home_r, part_s, part_r,
+    far_s, far_r, cross_s, cross_r, home_s, home_r, part_s, part_r, copy_sem,
 ):
     t = lax.axis_index("tower")
     c = lax.axis_index("grp")
@@ -187,6 +192,12 @@
             deliver(phase, gl, q_stage.at[phase * 4 + gl], q_here.at[phase * 4 + line.r],
                     q_s.at[phase * 4 + gl], q_r.at[phase * 4 + line.r])
 
+    stamps = jnp.broadcast_to(stamps_ref[...].astype(F32), (HEAD, TOK)).T
+    angles = stamps * frequency_ref[...]
+    column = lax.broadcasted_iota(jnp.int32, (TOK, HEAD), 1)
+    sine = jnp.sin(angles)
+    cos_ref[...] = jnp.cos(angles)
+    sin_ref[...] = jnp.where(column < HEAD // 2, -sine, sine)
     loads[0].wait()
     loads[1].wait()
     prepare_kv(0)
@@ -251,6 +262,11 @@
             number = int(name[3])
             step = (0, 3, 1, 2)[number]
             landed(blocks(phase, line.chunk(step, 1 - c), 4), sib_r.at[phase * 4 + number])
+        elif name == "near":
+            for step in (0, 1, 3):
+                copy_of(phase, step).start()
+        elif name == "rest":
+            copy_of(phase, 2).start()
         elif name == "cross":
             cross(phase)
         elif name == "finish":
@@ -258,44 +274,41 @@
         else:
             project(phase)
 
+    def copy_of(phase, step):
+        first = lines[ALONG_X[phase]].chunk(step, 0)
+        return pltpu.make_async_copy(
+            blocks(phase, first, 8), held.at[pl.ds(first, 8)], copy_sem.at[step]
+        )
+
     def cross(phase):
-        kind = 4 if ALONG_X[phase] else 0
-        want = [chosen_ref[kind + r] for r in range(4)]
-
-        def select(step, _):
-            rows = pl.ds(pl.multiple_of((step % 8) * 32, 32), 32)
-            which = step // 8
-            found = [jnp.zeros((32, HEAD), BF16) for r in range(4)]
-            for block in range(BLOCKS):
-                entries = kv[phase * BLOCKS + block, which, rows, :]
-                for r in range(4):
-                    found[r] = jnp.where(want[r] == block, entries, found[r])
-            for r in range(4):
-                picked[r, which, rows, :] = found[r]
-            return 0
-
-        lax.fori_loop(0, 16, select, 0)
+        line = lines[ALONG_X[phase]]
+        for step in range(4):
+            copy_of(phase, step).wait()
         landed(q_far.at[pl.ds(phase * 4, 4)], far_r.at[phase])
 
-        def one(r, _):
+        for r in range(4):
+            asked = place(line.along_x, line.u, 2 * c + r // 2, r % 2)
+            inverse = jnp.int32(0)
+            for k in range(BLOCKS):
+                inverse = jnp.where(partner_ref[k] == asked, k, inverse)
+            want = jnp.where(t == 1, partner_ref[asked], inverse)
+            if line.along_x:
+                want = ((want // 2) % 4) * 8 + (want // 8) * 2 + want % 2
             found = lax.dot_general(
-                q_far[phase * 4 + r], picked[r, 0], (((1,), (1,)), ((), ())),
+                q_far[phase * 4 + r], held[want, 0], (((1,), (1,)), ((), ())),
                 preferred_element_type=F32,
             ) * SCALE
             exponent = jnp.exp2(found - jnp.max(found, axis=1, keepdims=True))
             denominator = jnp.sum(exponent, axis=1, keepdims=True)
-            numerator = jnp.dot(exponent.astype(BF16), picked[r, 1], preferred_element_type=F32)
+            numerator = jnp.dot(exponent.astype(BF16), held[want, 1], preferred_element_type=F32)
             cross_mine[phase * 4 + r] = (numerator / denominator).astype(BF16)
-            return 0
-
-        lax.fori_loop(0, 4, one, 0)
-        remote(cross_mine.at[pl.ds(phase * 4, 4)], cross_far.at[pl.ds(phase * 4, 4)],
-               cross_s.at[phase], cross_r.at[phase], far).start()
+            remote(cross_mine.at[phase * 4 + r], cross_far.at[phase * 4 + r],
+                   cross_s.at[phase * 4 + r], cross_r.at[phase * 4 + r], far).start()
 
     def finish(phase):
         line = lines[ALONG_X[phase]]
-        landed(cross_far.at[pl.ds(phase * 4, 4)], cross_r.at[phase])
         for r in range(4):
+            landed(cross_far.at[phase * 4 + r], cross_r.at[phase * 4 + r])
             rows = pl.ds(phase * ROWS + r * TOK, TOK)
             own = acc[rows, 0:HEAD] / acc[rows, HEAD:]
             joined[phase * 4 + r] = (own + cross_far[phase * 4 + r].astype(F32)).astype(BF16)
@@ -380,6 +393,8 @@
 
     def events_of(pair, half):
         for number in range(len(ORDER)):
+            if isinstance(pair, int) and pair != number:
+                continue
             todo = slots.get(2 * number + half, [])
             if todo:
                 @pl.when(pair == number)
@@ -391,7 +406,7 @@
         event(name, phase)
     qk(phases[0], where_is(jnp.int32(phases[0]), jnp.int32(parts[0]), 0), 0)
 
-    def pair_step(pair, _):
+    def pair_step(pair, last=False):
         following = jnp.minimum(pair + 1, len(ORDER) - 1)
         phase, part = pick(pair, phases), pick(pair, parts)
         later_phase, later_part = pick(following, phases), pick(following, parts)
@@ -399,11 +414,13 @@
         qk(phase, where_is(phase, part, 1), 1)
         absorb(phase, where_is(phase, part, 0), 0)
         events_of(pair, 1)
-        qk(later_phase, where_is(later_phase, later_part, 0), 0)
+        if not last:
+            qk(later_phase, where_is(later_phase, later_part, 0), 0)
         absorb(phase, where_is(phase, part, 1), 1)
         return 0
 
-    lax.fori_loop(0, len(ORDER), pair_step, 0)
+    lax.fori_loop(0, len(ORDER) - 1, lambda pair, _: pair_step(pair), 0)
+    pair_step(jnp.int32(len(ORDER) - 1), last=True)
 
     finish(2)
     home_landed(2)
@@ -453,14 +470,14 @@
                 sent(joined.at[phase * 4 + number], home_s.at[phase * 4 + number])
 
             sent(blocks(phase, 0, 4), sib_s.at[phase * 4 + number])
+            sent(cross_mine.at[phase * 4 + number], cross_s.at[phase * 4 + number])
         for number in range(2):
             sent(blocks(phase, 0, 4), line_s.at[phase * 2 + number])
             sent(blocks(phase, 0, 2), opp_s.at[phase * 2 + number])
         sent(q_here.at[pl.ds(phase * 4, 4)], far_s.at[phase])
-        sent(cross_mine.at[pl.ds(phase * 4, 4)], cross_s.at[phase])
-
-
-def attention(queries, keys, values, cosine, sine, chosen, w_out):
+
+
+def attention(queries, keys, values, stamps, frequency, partner, w_out):
     dma = pltpu.SemaphoreType.DMA
     anywhere = pl.BlockSpec(memory_space=pl.ANY)
     vmem = pl.BlockSpec(memory_space=pltpu.VMEM)
@@ -473,6 +490,8 @@
                   pl.BlockSpec(memory_space=pltpu.SMEM), anywhere],
         out_specs=vmem,
         scratch_shapes=[
+            pltpu.VMEM((TOK, HEAD), F32),
+            pltpu.VMEM((TOK, HEAD), F32),
             pltpu.VMEM((TOK, HALF), BF16),
             pltpu.VMEM((TOK, HALF), BF16),
             pltpu.VMEM((TOK, HALF), BF16),
@@ -481,7 +500,7 @@
             pltpu.VMEM((heads, 2, TOK, HEAD), BF16),
             pltpu.VMEM((PHASES * BLOCKS, 2, TOK, HEAD), BF16),
             per_head, per_head, per_head, per_head,
-            pltpu.VMEM((4, 2, TOK, HEAD), BF16),
+            pltpu.VMEM((BLOCKS, 2, TOK, HEAD), BF16),
             per_head, per_head,
             pltpu.VMEM((TOK, MODEL), F32),
             pltpu.VMEM((TOK, HALF), BF16),
@@ -495,36 +514,21 @@
             dma((heads,)), dma((heads,)), dma((heads,)), dma((heads,)),
             dma((6,)), dma((6,)), dma((6,)), dma((6,)),
             dma((heads,)), dma((heads,)),
-            dma((3,)), dma((3,)), dma((3,)), dma((3,)),
+            dma((3,)), dma((3,)), dma((heads,)), dma((heads,)),
             dma((heads,)), dma((heads,)),
-            dma, dma,
+            dma, dma, dma((4,)),
         ],
         compiler_params=pltpu.CompilerParams(
             collective_id=0, has_side_effects=True, vmem_limit_bytes=63 * 2**20
         ),
-    )(queries, keys, values, cosine, sine, chosen, w_out)
+    )(queries, keys, values, stamps, frequency, partner, w_out)
 
 
 def body(queries, keys, values, stamps, partner, w_out):
     half_size = HEAD // 2
-    frequency = jnp.exp(-math.log(10000.0) * jnp.arange(half_size, dtype=F32) / half_size)
-    angles = stamps[0].astype(F32)[:, None] * frequency[None, :]
-    cosine, sine = jnp.cos(angles), jnp.sin(angles)
-    cosine = jnp.concatenate([cosine, cosine], axis=1)
-    sine = jnp.concatenate([-sine, sine], axis=1)
-    t, c, s = lax.axis_index("tower"), lax.axis_index("grp"), lax.axis_index("seq")
-    y, x = s // 8, (s // 2) % 4
-    r = jnp.arange(4, dtype=jnp.int32)
-    w, z = 2 * c + r // 2, r % 2
-    asked = jnp.concatenate([y * 8 + w * 2 + z, w * 8 + x * 2 + z])
-    shards = jnp.arange(BLOCKS, dtype=jnp.int32)[None, :]
-    given = partner[None, :]
-    forward = jnp.sum(jnp.where(shards == asked[:, None], given, 0), axis=1)
-    inverse = jnp.sum(jnp.where(given == asked[:, None], shards, 0), axis=1)
-    chosen = jnp.where(t == 1, forward, inverse)
-    swapped = ((chosen // 2) % 4) * 8 + (chosen // 8) * 2 + chosen % 2
-    chosen = jnp.where(jnp.arange(8) < 4, chosen, swapped).astype(jnp.int32)
-    return attention(queries, keys, values, cosine, sine, chosen, w_out)
+    frequency = np.exp(-math.log(10000.0) * np.arange(half_size) / half_size)
+    frequency = jnp.asarray(np.concatenate([frequency, frequency])[None, :], F32)
+    return attention(queries, keys, values, stamps, frequency, partner, w_out)
 
 
 def solution(mesh):

time: 112 us -> 99.2 us (0.89)
  Pallas kernels: 106 us -> 97 us
  other arithmetic: 3.58 us -> 0 us
    pallas_call x1, Pallas kernels: 106 us -> 97 us  [attention(): pl.pallas_call(kernel, out_shape=jax.ShapeDtypeStruct((1, TOK, HALF), BF1...]
where the time goes in v2:
time: 99.2 us; the launch traced here: 99.1 us
  Pallas kernels  97 us (98%)
  local copies, waits for them, and re-layouts  2.06 us (2%)
    pallas_call x1, Pallas kernels, attention(): pl.pallas_call(kernel, out_shape=jax.ShapeDtypeStruct((1, TOK, HALF), BF1...  97 us
    unnamed x1, local copies, waits for them, and re-layouts  2.06 us

profile of v2, /device:TPU:1, one launch (start us, length us, event | category | flops | bytes accessed | tf_op | source)
XLA Modules:
  0.0 99.1 jit_solution(10767486692198540066)
XLA Ops:
  0.0 97.0 %shard_map.73 = bf16[1,256,1536]{2,1,0:T(8,128)(2,1)} custom-call(bf16[1,256,1536]{2,1,0:T(8,128)(2,1)} %q_hbm.1, bf16[1,256,1536]{2,1,0:T(8,128)(2,1)} %k_hbm.1, bf16[1,256,1536]{2,1,0:T(8,128)(2,1)} %v_hbm.1, s32[1,256]{1,0:T(1,128)} %stamps_ref.1, f32[1,128]{1,0:T(1,128)} %constant.2.clone.frequency_ref, s32[32]{0:T(128)} %partner_ref.1, ...), custom_call_target="tpu_custom_call" | custom-call | tf_op jit(solution)/shard_map/pallas_call | solution.py:486
  97.0 2.1 %copy.9 = bf16[1,256,1536]{2,1,0:T(8,128)(2,1)} copy(bf16[1,256,1536]{2,1,0:T(8,128)(2,1)} %shard_map.73) | data formatting | bytes 1572864

commit v3 on v2

--- a/solution.py
+++ b/solution.py
@@ -207,9 +207,9 @@
     send_q(0)
     prepare_kv(1)
     send_kv(1)
-    send_q(1)
     prepare_kv(2)
     send_kv(2)
+    send_q(1)
     send_q(2)
 
     acc[...] = jnp.zeros(acc.shape, F32)

time: 99.2 us -> 99.2 us (level)
  no operation moved by 1% of the time
where the time goes in v3:
time: 99.2 us; the launch traced here: 99.1 us
  Pallas kernels  97 us (98%)
  local copies, waits for them, and re-layouts  2.06 us (2%)
    pallas_call x1, Pallas kernels, attention(): pl.pallas_call(kernel, out_shape=jax.ShapeDtypeStruct((1, TOK, HALF), BF1...  97 us
    unnamed x1, local copies, waits for them, and re-layouts  2.06 us

profile of v3, /device:TPU:1, one launch (start us, length us, event | category | flops | bytes accessed | tf_op | source)
XLA Modules:
  0.0 99.1 jit_solution(15126392518031460090)
XLA Ops:
  0.0 97.0 %shard_map.73 = bf16[1,256,1536]{2,1,0:T(8,128)(2,1)} custom-call(bf16[1,256,1536]{2,1,0:T(8,128)(2,1)} %q_hbm.1, bf16[1,256,1536]{2,1,0:T(8,128)(2,1)} %k_hbm.1, bf16[1,256,1536]{2,1,0:T(8,128)(2,1)} %v_hbm.1, s32[1,256]{1,0:T(1,128)} %stamps_ref.1, f32[1,128]{1,0:T(1,128)} %constant.2.clone.frequency_ref, s32[32]{0:T(128)} %partner_ref.1, ...), custom_call_target="tpu_custom_call" | custom-call | tf_op jit(solution)/shard_map/pallas_call | solution.py:486
  97.0 2.1 %copy.9 = bf16[1,256,1536]{2,1,0:T(8,128)(2,1)} copy(bf16[1,256,1536]{2,1,0:T(8,128)(2,1)} %shard_map.73) | data formatting | bytes 1572864

commit v4 on v3

--- a/solution.py
+++ b/solution.py
@@ -29,6 +29,7 @@
     (1, 1), (1, 2), (1, 3), (2, 1), (2, 2), (2, 3),
 )
 AHEAD = {
+    ("kv", 1): -1, ("q", 1): -1, ("kv", 2): -1, ("q", 2): -1,
     ("below", 1): 8, ("above", 1): 8,
     ("below", 2): 16, ("above", 2): 16,
     ("cross", 0): 11, ("finish", 0): 15, ("project", 0): 18,
@@ -56,7 +57,7 @@
         at[("rest", phase)] = at[("sib3", phase)]
     for key, place in AHEAD.items():
         at[key] = place if key not in at else min(place, at[key])
-    rank = ["ask", "own", "below", "above", "opposite", "sib0", "sib1", "sib2", "sib3",
+    rank = ["own", "kv", "q", "ask", "below", "above", "opposite", "sib0", "sib1", "sib2", "sib3",
             "near", "rest", "cross", "finish", "project"]
     slots = {}
     for (event, phase), place in sorted(at.items(), key=lambda e: (e[1], rank.index(e[0][0]), e[0][1])):
@@ -206,11 +207,7 @@
     loads[2].wait()
     send_q(0)
     prepare_kv(1)
-    send_kv(1)
     prepare_kv(2)
-    send_kv(2)
-    send_q(1)
-    send_q(2)
 
     acc[...] = jnp.zeros(acc.shape, F32)
     top[...] = jnp.full(top.shape, -1e30, F32)
@@ -267,6 +264,10 @@
                 copy_of(phase, step).start()
         elif name == "rest":
             copy_of(phase, 2).start()
+        elif name == "kv":
+            send_kv(phase)
+        elif name == "q":
+            send_q(phase)
         elif name == "cross":
             cross(phase)
         elif name == "finish":

time: 99.2 us -> 99.8 us (level)
  no operation moved by 1% of the time
where the time goes in v4:
time: 99.8 us; the launch traced here: 99.6 us
  Pallas kernels  97.5 us (98%)
  local copies, waits for them, and re-layouts  2.06 us (2%)
    pallas_call x1, Pallas kernels, attention(): pl.pallas_call(kernel, out_shape=jax.ShapeDtypeStruct((1, TOK, HALF), BF1...  97.5 us
    unnamed x1, local copies, waits for them, and re-layouts  2.06 us

profile of v4, /device:TPU:1, one launch (start us, length us, event | category | flops | bytes accessed | tf_op | source)
XLA Modules:
  0.0 99.6 jit_solution(7528199616478846505)
XLA Ops:
  0.0 97.5 %shard_map.73 = bf16[1,256,1536]{2,1,0:T(8,128)(2,1)} custom-call(bf16[1,256,1536]{2,1,0:T(8,128)(2,1)} %q_hbm.1, bf16[1,256,1536]{2,1,0:T(8,128)(2,1)} %k_hbm.1, bf16[1,256,1536]{2,1,0:T(8,128)(2,1)} %v_hbm.1, s32[1,256]{1,0:T(1,128)} %stamps_ref.1, f32[1,128]{1,0:T(1,128)} %constant.2.clone.frequency_ref, s32[32]{0:T(128)} %partner_ref.1, ...), custom_call_target="tpu_custom_call" | custom-call | tf_op jit(solution)/shard_map/pallas_call | solution.py:487
  97.5 2.1 %copy.9 = bf16[1,256,1536]{2,1,0:T(8,128)(2,1)} copy(bf16[1,256,1536]{2,1,0:T(8,128)(2,1)} %shard_map.73) | data formatting | bytes 1572864

commit v5 on v3

--- a/solution.py
+++ b/solution.py
@@ -25,7 +25,7 @@
 ALONG_X = (False, True, False)
 
 ORDER = (
-    (0, 0), (1, 0), (0, 1), (2, 0), (0, 2), (0, 3),
+    (0, 0), (1, 0), (2, 0), (0, 1), (0, 2), (0, 3),
     (1, 1), (1, 2), (1, 3), (2, 1), (2, 2), (2, 3),
 )
 AHEAD = {
@@ -49,14 +49,15 @@
         for event in NEEDS[(part, half)]:
             at[(event, phase)] = max(place - 1, -1)
             if event == "own":
-                at[("ask", phase)] = max(place - 1, -1)
+                at[("ask", phase)] = at[("line", phase)] = max(place - 1, -1)
+    at[("line", 2)] = at[("above", 0)]
     at[("cross", 2)] = at[("sib3", 2)]
     for phase in range(PHASES):
         at[("near", phase)] = at[("sib2", phase)]
         at[("rest", phase)] = at[("sib3", phase)]
     for key, place in AHEAD.items():
         at[key] = place if key not in at else min(place, at[key])
-    rank = ["ask", "own", "below", "above", "opposite", "sib0", "sib1", "sib2", "sib3",
+    rank = ["own", "ask", "below", "above", "line", "opposite", "sib0", "sib1", "sib2", "sib3",
             "near", "rest", "cross", "finish", "project"]
     slots = {}
     for (event, phase), place in sorted(at.items(), key=lambda e: (e[1], rank.index(e[0][0]), e[0][1])):
@@ -235,10 +236,11 @@
             first = line.chunk(0, c)
             for r in range(4):
                 landed(kv.at[phase * BLOCKS + first + r], kv_r.at[phase * 4 + r])
-            part = blocks(phase, first, 4)
+            to_sibling(phase, 0, blocks(phase, first, 4))
+        elif name == "line":
+            part = blocks(phase, line.chunk(0, c), 4)
             remote(part, part, line_s.at[phase * 2], line_r.at[phase * 2], line.next(1)).start()
             remote(part, part, line_s.at[phase * 2 + 1], line_r.at[phase * 2 + 1], line.next(3)).start()
-            to_sibling(phase, 0, part)
         elif name == "below":
             first = line.chunk(3, c)
             part = blocks(phase, first, 4)

time: 99.2 us -> 99 us (level)
  no operation moved by 1% of the time
where the time goes in v5:
time: 99 us; the launch traced here: 98.9 us
  Pallas kernels  96.8 us (98%)
  local copies, waits for them, and re-layouts  2.06 us (2%)
    pallas_call x1, Pallas kernels, attention(): pl.pallas_call(kernel, out_shape=jax.ShapeDtypeStruct((1, TOK, HALF), BF1...  96.8 us
    unnamed x1, local copies, waits for them, and re-layouts  2.06 us

profile of v5, /device:TPU:1, one launch (start us, length us, event | category | flops | bytes accessed | tf_op | source)
XLA Modules:
  0.0 98.9 jit_solution(14454261261276877646)
XLA Ops:
  0.0 96.8 %shard_map.73 = bf16[1,256,1536]{2,1,0:T(8,128)(2,1)} custom-call(bf16[1,256,1536]{2,1,0:T(8,128)(2,1)} %q_hbm.1, bf16[1,256,1536]{2,1,0:T(8,128)(2,1)} %k_hbm.1, bf16[1,256,1536]{2,1,0:T(8,128)(2,1)} %v_hbm.1, s32[1,256]{1,0:T(1,128)} %stamps_ref.1, f32[1,128]{1,0:T(1,128)} %constant.2.clone.frequency_ref, s32[32]{0:T(128)} %partner_ref.1, ...), custom_call_target="tpu_custom_call" | custom-call | tf_op jit(solution)/shard_map/pallas_call | solution.py:488
  96.8 2.1 %copy.9 = bf16[1,256,1536]{2,1,0:T(8,128)(2,1)} copy(bf16[1,256,1536]{2,1,0:T(8,128)(2,1)} %shard_map.73) | data formatting | bytes 1572864

commit v6 on v5

--- a/solution.py
+++ b/solution.py
@@ -29,6 +29,7 @@
     (1, 1), (1, 2), (1, 3), (2, 1), (2, 2), (2, 3),
 )
 AHEAD = {
+    ("own", 1): 0, ("line", 1): 0,
     ("below", 1): 8, ("above", 1): 8,
     ("below", 2): 16, ("above", 2): 16,
     ("cross", 0): 11, ("finish", 0): 15, ("project", 0): 18,
@@ -57,7 +58,7 @@
         at[("rest", phase)] = at[("sib3", phase)]
     for key, place in AHEAD.items():
         at[key] = place if key not in at else min(place, at[key])
-    rank = ["own", "ask", "below", "above", "line", "opposite", "sib0", "sib1", "sib2", "sib3",
+    rank = ["own", "line", "ask", "below", "above", "opposite", "sib0", "sib1", "sib2", "sib3",
             "near", "rest", "cross", "finish", "project"]
     slots = {}
     for (event, phase), place in sorted(at.items(), key=lambda e: (e[1], rank.index(e[0][0]), e[0][1])):
@@ -428,15 +429,14 @@
     home_landed(2)
     theirs, ours = (1 - c) * HALF, c * HALF
 
-    def for_sibling(n, _):
+    exchanges = []
+    for n in range(HALF // TILE):
         columns = pl.ds(pl.multiple_of(theirs + n * TILE, TILE), TILE)
-        here = pl.ds(pl.multiple_of(n * TILE, TILE), TILE)
-        part_out[:, here] = (total[:, columns] + product(2, columns)).astype(BF16)
-        return 0
-
-    lax.fori_loop(0, HALF // TILE, for_sibling, 0)
-    exchange = remote(part_out, part_in, part_s, part_r, sibling)
-    exchange.start()
+        part_out[n] = (total[:, columns] + product(2, columns)).astype(BF16)
+        exchanges.append(
+            remote(part_out.at[n], part_in.at[n], part_s.at[n], part_r.at[n], sibling)
+        )
+        exchanges[-1].start()
 
     def for_us(n, _):
         columns = pl.ds(pl.multiple_of(ours + n * TILE, TILE), TILE)
@@ -444,12 +444,13 @@
         return 0
 
     lax.fori_loop(0, HALF // TILE, for_us, 0)
-    exchange.wait()
+    for exchange in exchanges:
+        exchange.wait()
 
     def emit(n, _):
         columns = pl.ds(pl.multiple_of(ours + n * TILE, TILE), TILE)
         here = pl.ds(pl.multiple_of(n * TILE, TILE), TILE)
-        out_ref[0, :, here] = (total[:, columns] + part_in[:, here].astype(F32)).astype(BF16)
+        out_ref[0, :, here] = (total[:, columns] + part_in[n].astype(F32)).astype(BF16)
         return 0
 
     lax.fori_loop(0, HALF // TILE, emit, 0)
@@ -505,8 +506,8 @@
             pltpu.VMEM((BLOCKS, 2, TOK, HEAD), BF16),
             per_head, per_head,
             pltpu.VMEM((TOK, MODEL), F32),
-            pltpu.VMEM((TOK, HALF), BF16),
-            pltpu.VMEM((TOK, HALF), BF16),
+            pltpu.VMEM((HALF // TILE, TOK, TILE), BF16),
+            pltpu.VMEM((HALF // TILE, TOK, TILE), BF16),
             pltpu.VMEM((PHASES * ROWS, 2 * HEAD), F32),
             pltpu.VMEM((PHASES * ROWS, HEAD), F32),
             pltpu.VMEM((2, ROWS, HEAD), F32),
@@ -518,7 +519,7 @@
             dma((heads,)), dma((heads,)),
             dma((3,)), dma((3,)), dma((heads,)), dma((heads,)),
             dma((heads,)), dma((heads,)),
-            dma, dma, dma((4,)),
+            dma((HALF // TILE,)), dma((HALF // TILE,)), dma((4,)),
         ],
         compiler_params=pltpu.CompilerParams(
             collective_id=0, has_side_effects=True, vmem_limit_bytes=63 * 2**20

time: 99 us -> 109 us (1.10)
  Pallas kernels: 96.8 us -> 107 us
    pallas_call x1, Pallas kernels: 96.8 us -> 107 us  [attention(): pl.pallas_call(kernel, out_shape=jax.ShapeDtypeStruct((1, TOK, HALF), BF1...]
where the time goes in v6:
time: 109 us
  Pallas kernels  107 us (98%)
  local copies, waits for them, and re-layouts  2.06 us (2%)
    pallas_call x1, Pallas kernels, attention(): pl.pallas_call(kernel, out_shape=jax.ShapeDtypeStruct((1, TOK, HALF), BF1...  107 us

profile of v6, /device:TPU:1, one launch (start us, length us, event | category | flops | bytes accessed | tf_op | source)
XLA Modules:
  0.0 108.6 jit_solution(14925962207058663428)
XLA Ops:
  0.0 106.6 %shard_map.73 = bf16[1,256,1536]{2,1,0:T(8,128)(2,1)} custom-call(bf16[1,256,1536]{2,1,0:T(8,128)(2,1)} %q_hbm.1, bf16[1,256,1536]{2,1,0:T(8,128)(2,1)} %k_hbm.1, bf16[1,256,1536]{2,1,0:T(8,128)(2,1)} %v_hbm.1, s32[1,256]{1,0:T(1,128)} %stamps_ref.1, f32[1,128]{1,0:T(1,128)} %constant.2.clone.frequency_ref, s32[32]{0:T(128)} %partner_ref.1, ...), custom_call_target="tpu_custom_call" | custom-call | tf_op jit(solution)/shard_map/pallas_call | solution.py:489
  106.6 2.1 %copy.9 = bf16[1,256,1536]{2,1,0:T(8,128)(2,1)} copy(bf16[1,256,1536]{2,1,0:T(8,128)(2,1)} %shard_map.73) | data formatting | bytes 1572864

commit v7 on v6

--- a/solution.py
+++ b/solution.py
@@ -29,7 +29,6 @@
     (1, 1), (1, 2), (1, 3), (2, 1), (2, 2), (2, 3),
 )
 AHEAD = {
-    ("own", 1): 0, ("line", 1): 0,
     ("below", 1): 8, ("above", 1): 8,
     ("below", 2): 16, ("above", 2): 16,
     ("cross", 0): 11, ("finish", 0): 15, ("project", 0): 18,
@@ -51,6 +50,7 @@
             at[(event, phase)] = max(place - 1, -1)
             if event == "own":
                 at[("ask", phase)] = at[("line", phase)] = max(place - 1, -1)
+    at[("line", 1)] = at[("own", 2)]
     at[("line", 2)] = at[("above", 0)]
     at[("cross", 2)] = at[("sib3", 2)]
     for phase in range(PHASES):
@@ -58,7 +58,7 @@
         at[("rest", phase)] = at[("sib3", phase)]
     for key, place in AHEAD.items():
         at[key] = place if key not in at else min(place, at[key])
-    rank = ["own", "line", "ask", "below", "above", "opposite", "sib0", "sib1", "sib2", "sib3",
+    rank = ["own", "ask", "below", "above", "line", "opposite", "sib0", "sib1", "sib2", "sib3",
             "near", "rest", "cross", "finish", "project"]
     slots = {}
     for (event, phase), place in sorted(at.items(), key=lambda e: (e[1], rank.index(e[0][0]), e[0][1])):

time: 109 us -> 101 us (0.927)
  Pallas kernels: 107 us -> 99.1 us
    pallas_call x1, Pallas kernels: 107 us -> 99.1 us  [attention(): pl.pallas_call(kernel, out_shape=jax.ShapeDtypeStruct((1, TOK, HALF), BF1...]
where the time goes in v7:
time: 101 us
  Pallas kernels  99.1 us (98%)
  local copies, waits for them, and re-layouts  2.06 us (2%)
    pallas_call x1, Pallas kernels, attention(): pl.pallas_call(kernel, out_shape=jax.ShapeDtypeStruct((1, TOK, HALF), BF1...  99.1 us
    unnamed x1, local copies, waits for them, and re-layouts  2.06 us

profile of v7, /device:TPU:1, one launch (start us, length us, event | category | flops | bytes accessed | tf_op | source)
XLA Modules:
  0.0 101.1 jit_solution(8933976135937235745)
XLA Ops:
  0.0 99.1 %shard_map.73 = bf16[1,256,1536]{2,1,0:T(8,128)(2,1)} custom-call(bf16[1,256,1536]{2,1,0:T(8,128)(2,1)} %q_hbm.1, bf16[1,256,1536]{2,1,0:T(8,128)(2,1)} %k_hbm.1, bf16[1,256,1536]{2,1,0:T(8,128)(2,1)} %v_hbm.1, s32[1,256]{1,0:T(1,128)} %stamps_ref.1, f32[1,128]{1,0:T(1,128)} %constant.2.clone.frequency_ref, s32[32]{0:T(128)} %partner_ref.1, ...), custom_call_target="tpu_custom_call" | custom-call | tf_op jit(solution)/shard_map/pallas_call | solution.py:489
  99.1 2.1 %copy.9 = bf16[1,256,1536]{2,1,0:T(8,128)(2,1)} copy(bf16[1,256,1536]{2,1,0:T(8,128)(2,1)} %shard_map.73) | data formatting | bytes 1572864
